TPU v7x, 32 devices: a whole 2x2x4 slice. The times are simulated.
32 devices in a mesh: freq: 8 (over z, y), pencil: 4 (over x, core).
Axes of the slice: x: 2, y: 2, z: 4, core: 2. Of those that a mesh axis runs over, the one named last changes fastest.
Arguments:
- wave_field: float32 [16, 512, 2, 512], P('freq', 'pencil'), may hold values from -6 to 6
- source_field: float32 [1, 16, 512, 2, 512], P(None, 'freq', 'pencil'), may hold values from -6 to 6
- omegas: float32 [16], P('freq'), may hold values from 30 to 250
- velocities: float32 [1, 6], replicated, may hold values from 1500 to 4500
- lower_ref: int32 [1, 8, 8], replicated, may hold values from 0 to 4, as said below
- blend_weight: float32 [1, 8, 8], replicated, may hold values from 0 to 1
Outputs:
- new_field: float32 [16, 512, 2, 512], P('freq', 'pencil')
- image: float32 [1, 512, 512], P(None, 'pencil', 'freq')
Inputs may be any that keep to these rules, and one draw needn't show every extreme that they name: `lower_ref`: in each depth step the lower references of one tile row differ by at most one, so a tile row's tiles use at most three consecutive references; in each depth step one tile row uses references 0 to 2 and another references 6 - 3 to 5.
All inputs are finite; a program needn't handle non-finite values.
Results may differ from a plain program's by a relative error of at most 0.0001.
Values sent between devices are 32-bit elements; how exact they have to be, the bound alone decides.
A program may use at most 128 MiB of HBM per device.

v0:
```python
import math

import jax
import jax.numpy as jnp
from jax import lax
from jax.sharding import PartitionSpec as P

TILE = 64


GRID_SPACING = 12.5
DEPTH_STEP = 10.0


def wave_numbers(amount, offset, length):
    index_all = offset + jnp.arange(amount, dtype=jnp.int32)
    signed = jnp.where(index_all < length // 2, index_all, index_all - length)
    return signed.astype(jnp.float32) * (2.0 * math.pi / (length * GRID_SPACING))


def phase_terms(angular, velocity, radial):
    vertical = (angular / velocity) ** 2 - radial
    travel = jnp.sqrt(jnp.maximum(vertical, 0.0)) * DEPTH_STEP
    damping = jnp.exp(-jnp.sqrt(jnp.maximum(-vertical, 0.0)) * DEPTH_STEP)
    return (damping * jnp.cos(travel), damping * jnp.sin(travel))


def tile_coefficients(lower_idx, weight, ref_value):
    return jnp.where(lower_idx == ref_value, weight, 0.0) + jnp.where(
        lower_idx + 1 == ref_value, 1.0 - weight, 0.0
    )


def fourier_tables(length):
    index_all = jnp.arange(length, dtype=jnp.int32)
    product = index_all[:, None] * index_all[None, :] % length
    angles = product.astype(jnp.float32) * (2.0 * math.pi / length)
    norming = 1.0 / math.sqrt(length)
    return (jnp.cos(angles) * norming, jnp.sin(angles) * norming)


def along_last(values, matrix):
    return jnp.einsum(
        "...n,nk->...k",
        values,
        matrix,
        precision=lax.Precision.HIGHEST,
        preferred_element_type=jnp.float32,
    )


def along_rows(matrix, values):
    return jnp.einsum(
        "kn,fnj->fkj",
        matrix,
        values,
        precision=lax.Precision.HIGHEST,
        preferred_element_type=jnp.float32,
    )


def on_device(wave_field, source_field, omegas, velocities, lower_ref, blend_weight):
    pencils = lax.axis_size("pencil")
    position = lax.axis_index("pencil")
    groups = lax.axis_size("freq")
    freq_count = wave_field.shape[0]
    own_rows = wave_field.shape[1]
    width_y = wave_field.shape[3]
    width_x = own_rows * pencils
    own_cols = width_y // pencils
    own_bands = own_rows // TILE
    cos_y, sin_y = fourier_tables(width_y)
    cos_x, sin_x = fourier_tables(width_x)
    radial = (
        wave_numbers(width_x, 0, width_x)[:, None] ** 2
        + wave_numbers(own_cols, position * own_cols, width_y)[None, :] ** 2
    )
    image_scale = 1.0 / math.sqrt(freq_count * groups)
    wavefield = wave_field
    real_part = wavefield[:, :, 0]
    imag_part = wavefield[:, :, 1]
    spec_real = along_last(real_part, cos_y) + along_last(imag_part, sin_y)
    spec_imag = along_last(imag_part, cos_y) - along_last(real_part, sin_y)
    columns = lax.all_to_all(
        jnp.stack([spec_real, spec_imag], axis=2), "pencil", split_axis=3, concat_axis=1, tiled=True
    )
    col_real = columns[:, :, 0]
    col_imag = columns[:, :, 1]
    wave_real = along_rows(cos_x, col_real) + along_rows(sin_x, col_imag)
    wave_imag = along_rows(cos_x, col_imag) - along_rows(sin_x, col_real)
    speeds = velocities[0]
    lower_own = lax.dynamic_slice_in_dim(lower_ref[0], position * own_bands, own_bands, 0)
    weight_own = lax.dynamic_slice_in_dim(blend_weight[0], position * own_bands, own_bands, 0)
    shifted_all = []
    for ref_index in range(speeds.shape[0]):
        cos_part, sin_part = phase_terms(omegas[:, None, None], speeds[ref_index], radial[None])
        shift_real = wave_real * cos_part - wave_imag * sin_part
        shift_imag = wave_real * sin_part + wave_imag * cos_part
        back_real = along_rows(cos_x, shift_real) - along_rows(sin_x, shift_imag)
        back_imag = along_rows(cos_x, shift_imag) + along_rows(sin_x, shift_real)
        shifted_all.append(jnp.stack([back_real, back_imag], axis=2))
    arrived = lax.all_to_all(
        jnp.stack(shifted_all, axis=1), "pencil", split_axis=2, concat_axis=4, tiled=True
    )
    space_real = along_last(arrived[:, :, :, 0], cos_y) - along_last(arrived[:, :, :, 1], sin_y)
    space_imag = along_last(arrived[:, :, :, 1], cos_y) + along_last(arrived[:, :, :, 0], sin_y)
    lower_pix = jnp.repeat(jnp.repeat(lower_own, TILE, axis=0), TILE, axis=1)
    weight_pix = jnp.repeat(jnp.repeat(weight_own, TILE, axis=0), TILE, axis=1)
    ref_coef = jnp.stack(
        [
            tile_coefficients(lower_pix, weight_pix, ref_index)
            for ref_index in range(speeds.shape[0])
        ]
    )
    new_real = jnp.sum(ref_coef[None] * space_real, axis=1)
    new_imag = jnp.sum(ref_coef[None] * space_imag, axis=1)
    wavefield = jnp.stack([new_real, new_imag], axis=2)
    source = source_field[0]
    partial_image = (
        jnp.sum(source[:, :, 0] * new_real + source[:, :, 1] * new_imag, axis=0) * image_scale
    )
    images = [lax.psum_scatter(partial_image, "freq", scatter_dimension=1, tiled=True)]
    return (wavefield, jnp.stack(images))


def solution(mesh):
    placed = (
        P("freq", "pencil", None, None),
        P(None, "freq", "pencil", None, None),
        P("freq"),
        P(),
        P(),
        P(),
    )
    return jax.shard_map(
        on_device,
        mesh=mesh,
        in_specs=placed,
        out_specs=(P("freq", "pencil", None, None), P(None, "pencil", "freq")),
        check_vma=False,
    )
```

profile of v0, /device:TPU:0, one launch (start us, length us, event | category | flops | bytes accessed | tf_op | source)
XLA Modules:
  0.0 450.8 jit_solution(16425448492579560500)
XLA Ops:
  7.2 2.5 fusion.340
  9.7 5.6 %fusion.79 = f32[512,2,128]{2,0,1:T(8,128)S(1)} fusion(f32[2,128,1,512]{3,2,1,0:T(1,128)S(1)} %get-tuple-element.34), kind=kOutput, calls=%fused_computation.111 | convolution fusion | flops 809238528 | bytes 1048576 | tf_op jit(solution)/shard_map/...n,nk->...k/dot_general | solution.py:43
  15.3 5.8 %fusion.77 = f32[512,2,128]{2,0,1:T(8,128)S(1)} fusion(f32[2,128,1,512]{3,2,1,0:T(1,128)S(1)} %get-tuple-element.35), kind=kOutput, calls=%fused_computation.109 | convolution fusion | flops 809238528 | bytes 1048576 | tf_op jit(solution)/shard_map/...n,nk->...k/dot_general | solution.py:43
  21.1 5.6 %fusion.19 = f32[2,128,1,512]{1,3,0,2:T(8,128)S(1)} fusion(f32[512,2,128]{2,0,1:T(8,128)S(1)} %fusion.79, f32[2,128,1,512]{3,2,1,0:T(1,128)S(1)} %get-tuple-element.35), kind=kOutput, calls=%fused_computation.43 | convolution fusion | flops 809369600 | bytes 1572864 | tf_op jit(solution)/shard_map/...n,nk->...k/dot_general | solution.py:43
  26.8 15.2 %fusion.18 = f32[2,128,1,512]{1,3,0,2:T(8,128)S(1)} fusion(f32[512,2,128]{2,0,1:T(8,128)S(1)} %fusion.77, f32[2,128,1,512]{3,2,1,0:T(1,128)S(1)} %get-tuple-element.34), kind=kOutput, calls=%fused_computation.41 | convolution fusion | flops 809369600 | bytes 1572864 | tf_op jit(solution)/shard_map/...n,nk->...k/dot_general | solution.py:43
  42.1 1.8 copy.113
  43.9 4.2 all-to-all-start
  48.1 0.7 fusion.341
  48.8 3.8 divide_multiply_fusion
  52.7 9.9 %all-to-all-done = f32[2,128,2,512]{1,0,2,3:T(2,128)S(1)} async-done(((f32[2,128,2,512]{1,0,2,3:T(2,128)}), f32[2,128,2,512]{1,0,2,3:T(2,128)S(1)}, u32[]{:S(2)}, u32[]{:S(2)}) %all-to-all-start) | async-done | bytes 1048608 | tf_op jit(solution)/shard_map/all_to_all | solution.py:84
  62.6 0.7 copy.145
  63.3 0.4 all_to_all.29
  63.7 4.9 %fusion.75 = f32[2,128,512]{2,1,0:T(8,128)S(1)} fusion(f32[2,512,2,128]{1,3,0,2:T(8,128)S(1)} %all_to_all.29), kind=kOutput, calls=%fused_computation.107 | convolution fusion | flops 809238528 | bytes 1048576 | tf_op jit(solution)/shard_map/kn,fnj->fkj/dot_general | solution.py:53
  68.6 4.9 %fusion.73 = f32[2,128,512]{2,1,0:T(8,128)S(1)} fusion(f32[2,512,2,128]{1,3,0,2:T(8,128)S(1)} %all_to_all.29), kind=kOutput, calls=%fused_computation.105 | convolution fusion | flops 809238528 | bytes 1048576 | tf_op jit(solution)/shard_map/kn,fnj->fkj/dot_general | solution.py:53
  73.5 5.4 %fusion.17 = f32[2,512,128]{1,2,0:T(8,128)S(1)} fusion(f32[2,128,512]{2,1,0:T(8,128)S(1)} %fusion.75, f32[2,512,2,128]{1,3,0,2:T(8,128)S(1)} %all_to_all.29), kind=kOutput, calls=%fused_computation.39 | convolution fusion | flops 809369600 | bytes 1572864 | tf_op jit(solution)/shard_map/kn,fnj->fkj/dot_general | solution.py:53
  78.9 19.0 %multiply_subtract_fusion = (f32[2,512,128]{1,2,0:T(8,128)S(1)}, f32[2,512,128]{1,2,0:T(8,128)S(1)}, f32[2,512,128]{1,2,0:T(8,128)S(1)}, f32[2,512,128]{1,2,0:T(...) fusion(f32[2,512,128]{1,2,0:T(8,128)S(1)} %fusion.17, ...), kind=kOutput, calls=%fused_computation.209 | convolution fusion | flops 821166080 | bytes 8129536 | tf_op jit(solution)/shard_map/kn,fnj->fkj/dot_general | solution.py:53
  97.9 5.5 %fusion.67 = f32[2,128,512]{2,1,0:T(8,128)S(1)} fusion(f32[2,512,128]{1,2,0:T(8,128)S(1)} %get-tuple-element.31), kind=kOutput, calls=%fused_computation.99 | convolution fusion | flops 809238528 | bytes 1048576 | tf_op jit(solution)/shard_map/kn,fnj->fkj/dot_general | solution.py:53
  103.4 5.4 %fusion.65 = f32[2,128,512]{2,1,0:T(8,128)S(1)} fusion(f32[2,512,128]{1,2,0:T(8,128)S(1)} %get-tuple-element.30), kind=kOutput, calls=%fused_computation.97 | convolution fusion | flops 809238528 | bytes 1048576 | tf_op jit(solution)/shard_map/kn,fnj->fkj/dot_general | solution.py:53
  108.8 5.4 %fusion.13 = f32[2,512,1,128]{1,3,0,2:T(8,128)S(1)} fusion(f32[2,128,512]{2,1,0:T(8,128)S(1)} %fusion.67, f32[2,512,128]{1,2,0:T(8,128)S(1)} %get-tuple-element.30), kind=kOutput, calls=%fused_computation.31 | convolution fusion | flops 809369600 | bytes 1572864 | tf_op jit(solution)/shard_map/kn,fnj->fkj/dot_general | solution.py:53
  114.1 5.4 %fusion.12 = f32[2,512,1,128]{1,3,0,2:T(8,128)S(1)} fusion(f32[2,128,512]{2,1,0:T(8,128)S(1)} %fusion.65, f32[2,512,128]{1,2,0:T(8,128)S(1)} %get-tuple-element.31), kind=kOutput, calls=%fused_computation.29 | convolution fusion | flops 809369600 | bytes 1572864 | tf_op jit(solution)/shard_map/kn,fnj->fkj/dot_general | solution.py:53
  119.5 5.6 %fusion.71 = f32[2,128,512]{2,1,0:T(8,128)S(1)} fusion(f32[2,512,128]{1,2,0:T(8,128)S(1)} %get-tuple-element.33), kind=kOutput, calls=%fused_computation.103 | convolution fusion | flops 809238528 | bytes 1048576 | tf_op jit(solution)/shard_map/kn,fnj->fkj/dot_general | solution.py:53
  125.1 5.4 %fusion.69 = f32[2,128,512]{2,1,0:T(8,128)S(1)} fusion(f32[2,512,128]{1,2,0:T(8,128)S(1)} %get-tuple-element.32), kind=kOutput, calls=%fused_computation.101 | convolution fusion | flops 809238528 | bytes 1048576 | tf_op jit(solution)/shard_map/kn,fnj->fkj/dot_general | solution.py:53
  130.4 5.4 %fusion.15 = f32[2,512,1,128]{1,3,0,2:T(8,128)S(1)} fusion(f32[2,128,512]{2,1,0:T(8,128)S(1)} %fusion.71, f32[2,512,128]{1,2,0:T(8,128)S(1)} %get-tuple-element.32), kind=kOutput, calls=%fused_computation.35 | convolution fusion | flops 809369600 | bytes 1572864 | tf_op jit(solution)/shard_map/kn,fnj->fkj/dot_general | solution.py:53
  135.8 5.4 %fusion.14 = f32[2,512,1,128]{1,3,0,2:T(8,128)S(1)} fusion(f32[2,128,512]{2,1,0:T(8,128)S(1)} %fusion.69, f32[2,512,128]{1,2,0:T(8,128)S(1)} %get-tuple-element.33), kind=kOutput, calls=%fused_computation.33 | convolution fusion | flops 809369600 | bytes 1572864 | tf_op jit(solution)/shard_map/kn,fnj->fkj/dot_general | solution.py:53
  141.2 5.7 %fusion.61 = f32[2,128,512]{2,1,0:T(8,128)S(1)} fusion(f32[2,512,128]{1,2,0:T(8,128)S(1)} %get-tuple-element.28), kind=kOutput, calls=%fused_computation.93 | convolution fusion | flops 809238528 | bytes 1048576 | tf_op jit(solution)/shard_map/kn,fnj->fkj/dot_general | solution.py:53
  147.0 5.3 %fusion.63 = f32[2,128,512]{2,1,0:T(8,128)S(1)} fusion(f32[2,512,128]{1,2,0:T(8,128)S(1)} %get-tuple-element.29), kind=kOutput, calls=%fused_computation.95 | convolution fusion | flops 809238528 | bytes 1048576 | tf_op jit(solution)/shard_map/kn,fnj->fkj/dot_general | solution.py:53
  152.3 5.4 %fusion.10 = f32[2,512,1,128]{1,3,0,2:T(8,128)S(1)} fusion(f32[2,128,512]{2,1,0:T(8,128)S(1)} %fusion.61, f32[2,512,128]{1,2,0:T(8,128)S(1)} %get-tuple-element.29), kind=kOutput, calls=%fused_computation.25 | convolution fusion | flops 809369600 | bytes 1572864 | tf_op jit(solution)/shard_map/kn,fnj->fkj/dot_general | solution.py:53
  157.7 5.4 %fusion.11 = f32[2,512,1,128]{1,3,0,2:T(8,128)S(1)} fusion(f32[2,128,512]{2,1,0:T(8,128)S(1)} %fusion.63, f32[2,512,128]{1,2,0:T(8,128)S(1)} %get-tuple-element.28), kind=kOutput, calls=%fused_computation.27 | convolution fusion | flops 809369600 | bytes 1572864 | tf_op jit(solution)/shard_map/kn,fnj->fkj/dot_general | solution.py:53
  163.1 5.5 %fusion.57 = f32[2,128,512]{2,1,0:T(8,128)S(1)} fusion(f32[2,512,128]{1,2,0:T(8,128)S(1)} %get-tuple-element.26), kind=kOutput, calls=%fused_computation.89 | convolution fusion | flops 809238528 | bytes 1048576 | tf_op jit(solution)/shard_map/kn,fnj->fkj/dot_general | solution.py:53
  168.6 5.4 %fusion.59 = f32[2,128,512]{2,1,0:T(8,128)S(1)} fusion(f32[2,512,128]{1,2,0:T(8,128)S(1)} %get-tuple-element.27), kind=kOutput, calls=%fused_computation.91 | convolution fusion | flops 809238528 | bytes 1048576 | tf_op jit(solution)/shard_map/kn,fnj->fkj/dot_general | solution.py:53
  174.0 5.4 %fusion.8 = f32[2,512,1,128]{1,3,0,2:T(8,128)S(1)} fusion(f32[2,128,512]{2,1,0:T(8,128)S(1)} %fusion.57, f32[2,512,128]{1,2,0:T(8,128)S(1)} %get-tuple-element.27), kind=kOutput, calls=%fused_computation.21 | convolution fusion | flops 809369600 | bytes 1572864 | tf_op jit(solution)/shard_map/kn,fnj->fkj/dot_general | solution.py:53
  179.3 5.4 %fusion.9 = f32[2,512,1,128]{1,3,0,2:T(8,128)S(1)} fusion(f32[2,128,512]{2,1,0:T(8,128)S(1)} %fusion.59, f32[2,512,128]{1,2,0:T(8,128)S(1)} %get-tuple-element.26), kind=kOutput, calls=%fused_computation.23 | convolution fusion | flops 809369600 | bytes 1572864 | tf_op jit(solution)/shard_map/kn,fnj->fkj/dot_general | solution.py:53
  184.7 5.8 %fusion.53 = f32[2,128,512]{2,1,0:T(8,128)S(1)} fusion(f32[2,512,128]{1,2,0:T(8,128)S(1)} %get-tuple-element.24), kind=kOutput, calls=%fused_computation.85 | convolution fusion | flops 809238528 | bytes 1048576 | tf_op jit(solution)/shard_map/kn,fnj->fkj/dot_general | solution.py:53
  190.5 5.4 %fusion.55 = f32[2,128,512]{2,1,0:T(8,128)S(1)} fusion(f32[2,512,128]{1,2,0:T(8,128)S(1)} %get-tuple-element.25), kind=kOutput, calls=%fused_computation.87 | convolution fusion | flops 809238528 | bytes 1048576 | tf_op jit(solution)/shard_map/kn,fnj->fkj/dot_general | solution.py:53
  195.8 5.4 %fusion.6 = f32[2,512,1,128]{1,3,0,2:T(8,128)S(1)} fusion(f32[2,128,512]{2,1,0:T(8,128)S(1)} %fusion.53, f32[2,512,128]{1,2,0:T(8,128)S(1)} %get-tuple-element.25), kind=kOutput, calls=%fused_computation.17 | convolution fusion | flops 809369600 | bytes 1572864 | tf_op jit(solution)/shard_map/kn,fnj->fkj/dot_general | solution.py:53
  201.2 5.4 %fusion.7 = f32[2,512,1,128]{1,3,0,2:T(8,128)S(1)} fusion(f32[2,128,512]{2,1,0:T(8,128)S(1)} %fusion.55, f32[2,512,128]{1,2,0:T(8,128)S(1)} %get-tuple-element.24), kind=kOutput, calls=%fused_computation.19 | convolution fusion | flops 809369600 | bytes 1572864 | tf_op jit(solution)/shard_map/kn,fnj->fkj/dot_general | solution.py:53
  206.6 5.5 %fusion.49 = f32[2,128,512]{2,1,0:T(8,128)S(1)} fusion(f32[2,512,128]{1,2,0:T(8,128)S(1)} %get-tuple-element.13), kind=kOutput, calls=%fused_computation.81 | convolution fusion | flops 809238528 | bytes 1048576 | tf_op jit(solution)/shard_map/kn,fnj->fkj/dot_general | solution.py:53
  212.1 5.4 %fusion.51 = f32[2,128,512]{2,1,0:T(8,128)S(1)} fusion(f32[2,512,128]{1,2,0:T(8,128)S(1)} %get-tuple-element.12), kind=kOutput, calls=%fused_computation.83 | convolution fusion | flops 809238528 | bytes 1048576 | tf_op jit(solution)/shard_map/kn,fnj->fkj/dot_general | solution.py:53
  217.5 5.4 %fusion.4 = f32[2,512,1,128]{1,3,0,2:T(8,128)S(1)} fusion(f32[2,128,512]{2,1,0:T(8,128)S(1)} %fusion.49, f32[2,512,128]{1,2,0:T(8,128)S(1)} %get-tuple-element.12), kind=kOutput, calls=%fused_computation.13 | convolution fusion | flops 809369600 | bytes 1572864 | tf_op jit(solution)/shard_map/kn,fnj->fkj/dot_general | solution.py:53
  222.9 5.4 %fusion.5 = f32[2,512,1,128]{1,3,0,2:T(8,128)S(1)} fusion(f32[2,128,512]{2,1,0:T(8,128)S(1)} %fusion.51, f32[2,512,128]{1,2,0:T(8,128)S(1)} %get-tuple-element.13), kind=kOutput, calls=%fused_computation.15 | convolution fusion | flops 809369600 | bytes 1572864 | tf_op jit(solution)/shard_map/kn,fnj->fkj/dot_general | solution.py:53
  228.2 1.0 fusion.23
  229.3 1.1 fusion.24
  230.4 1.1 fusion.25
  231.4 1.1 fusion.26
  232.5 1.0 fusion.27
  233.5 1.1 fusion.28
  234.6 10.3 %copy.115 = f32[2,6,512,2,128]{4,0,3,1,2:T(2,128)} copy(f32[2,6,512,2,128]{2,4,0,3,1:T(8,128)} %fusion.28) | data formatting | bytes 12582912 | tf_op jit(solution)/shard_map/stack | solution.py:103
  244.9 5.2 %all-to-all-start.1 = ((f32[2,6,512,2,128]{4,0,3,1,2:T(2,128)}), f32[2,6,512,2,128]{4,0,3,1,2:T(2,128)}, u32[]{:S(2)}, u32[]{:S(2)}) async-start(f32[2,6,512,2,128]{4,0,3,1,2:T(2,128)} %copy.115), calls=%async_computation.1 | async-start | bytes 12582912 | tf_op jit(solution)/shard_map/all_to_all | solution.py:102
  250.2 0.7 compare_bitcast_fusion.1
  254.7 0.5 copy.106
  255.1 2.4 copy.144
  257.5 63.3 %all-to-all-done.1 = f32[2,6,512,2,128]{4,0,3,1,2:T(2,128)} async-done(((f32[2,6,512,2,128]{4,0,3,1,2:T(2,128)}), f32[2,6,512,2,128]{4,0,3,1,2:T(2,128)}, u32[]{:S(2)}, u32[]{:S(2)}) %all-to-all-start.1) | async-done | bytes 6291488 | tf_op jit(solution)/shard_map/all_to_all | solution.py:102
  320.9 9.5 %copy.143 = f32[2,6,4,128,2,128]{5,2,3,1,0,4:T(4,128)} copy(f32[2,6,4,128,2,128]{5,0,4,1,3,2:T(2,128)} %bitcast.73) | data formatting | bytes 12582912 | tf_op jit(solution)/shard_map/all_to_all | solution.py:102
  330.3 8.3 %all_to_all.33 = f32[2,6,128,2,512]{4,2,1,0,3:T(8,128)} reshape(f32[2,6,128,2,4,128]{5,4,2,1,0,3:T(4,128)} %bitcast.322) | data formatting | bytes 12582912 | tf_op jit(solution)/shard_map/all_to_all | solution.py:102
  338.6 11.3 %fusion.1 = f32[2,6,128,512]{3,2,1,0:T(8,128)S(1)} fusion(f32[2,6,128,2,512]{4,2,1,0,3:T(8,128)} %all_to_all.33), kind=kOutput, calls=%fused_computation.6 | convolution fusion | flops 4835770368 | bytes 6291456 | tf_op jit(solution)/shard_map/...n,nk->...k/dot_general | solution.py:43
  349.9 9.5 %fusion = f32[2,6,128,512]{3,2,1,0:T(8,128)S(1)} fusion(f32[2,6,128,2,512]{4,2,1,0,3:T(8,128)S(1)} %copy-done.1), kind=kOutput, calls=%fused_computation.5 | convolution fusion | flops 4835770368 | bytes 6291456 | tf_op jit(solution)/shard_map/...n,nk->...k/dot_general | solution.py:43
  359.4 9.5 %multiply_reduce_fusion.1 = f32[2,128,512]{2,1,0:T(8,128)S(1)} fusion(f32[2,6,128,512]{3,2,1,0:T(8,128)S(1)} %fusion.1, f32[6,128,512]{2,1,0:T(8,128)S(1)} %copy.106, f32[2,6,128,2,512]{4,2,1,0,3:T(8,128)S(1)} %copy-done.1), kind=kOutput, calls=%fused_computation.4 | convolution fusion | flops 4837998592 | bytes 8388608 | tf_op jit(solution)/shard_map/...n,nk->...k/dot_general | solution.py:43
  369.0 9.6 %multiply_reduce_fusion = f32[2,128,512]{2,1,0:T(8,128)S(1)} fusion(f32[2,6,128,512]{3,2,1,0:T(8,128)S(1)} %fusion, f32[6,128,512]{2,1,0:T(8,128)S(1)} %copy.106, f32[2,6,128,2,512]{4,2,1,0,3:T(8,128)S(1)} %copy-done.1), kind=kOutput, calls=%fused_computation.3 | convolution fusion | flops 4837998592 | bytes 8388608 | tf_op jit(solution)/shard_map/...n,nk->...k/dot_general | solution.py:43
  378.6 0.2 fusion.152
  378.9 0.8 copy.130
  379.8 1.8 copy.118
  381.6 60.6 %reduce-scatter.4.cloned.1.call-done = f32[64,128]{1,0:T(8,128)} async-done(((f32[512,128]{1,0:T(8,128)}), f32[64,128]{1,0:T(8,128)}) %reduce-scatter.4.cloned.1.call-update) | async-done | bytes 32784
  442.2 0.8 copy.131
  443.0 0.7 copy.119
  (67 shorter events, 4.1 us)
Async XLA Ops:
  7.2 246.7 %copy-start = (f32[1,8,8]{2,1,0:T(8,128)S(1)}, f32[1,8,8]{2,1,0:T(8,128)}, u32[]{:S(2)}) copy-start(f32[1,8,8]{2,1,0:T(8,128)} %param.11) | copy-start | bytes 772
  42.0 6.2 %copy-start.3 = (f32[1,6]{1,0:T(1,128)S(1)}, f32[1,6]{1,0:T(1,128)}, u32[]{:S(2)}) copy-start(f32[1,6]{1,0:T(1,128)} %param.9) | copy-start | bytes 76
  42.0 6.8 %copy-start.4 = (f32[2]{0:T(128)S(1)}, f32[2]{0:T(128)}, u32[]{:S(2)}) copy-start(f32[2]{0:T(128)} %param.8) | copy-start | bytes 28
  43.9 18.7 %all-to-all-start = ((f32[2,128,2,512]{1,0,2,3:T(2,128)}), f32[2,128,2,512]{1,0,2,3:T(2,128)S(1)}, u32[]{:S(2)}, u32[]{:S(2)}) async-start(f32[2,128,2,512]{1,0,2,3:T(2,128)} %copy.113), calls=%async_computation | async-start | bytes 2097152 | tf_op jit(solution)/shard_map/all_to_all | solution.py:84
  244.9 75.9 %all-to-all-start.1 = ((f32[2,6,512,2,128]{4,0,3,1,2:T(2,128)}), f32[2,6,512,2,128]{4,0,3,1,2:T(2,128)}, u32[]{:S(2)}, u32[]{:S(2)}) async-start(f32[2,6,512,2,128]{4,0,3,1,2:T(2,128)} %copy.115), calls=%async_computation.1 | async-start | bytes 12582912 | tf_op jit(solution)/shard_map/all_to_all | solution.py:102
  250.2 192.0 %reduce-scatter.4.cloned.1.call-start = ((), (), s32[]{:S(2)}) async-start(), calls=%async_computation.3 | async-start | bytes 294912
  338.6 11.3 %copy-start.1 = (f32[2,6,128,2,512]{4,2,1,0,3:T(8,128)S(1)}, f32[2,6,128,2,512]{4,2,1,0,3:T(8,128)}, u32[]{:S(2)}) copy-start(f32[2,6,128,2,512]{4,2,1,0,3:T(8,128)} %all_to_all.33) | copy-start | bytes 18874372
  369.0 9.7 %copy-start.2 = (f32[1,2,128,2,512]{4,2,1,3,0:T(8,128)S(1)}, f32[1,2,128,2,512]{4,2,1,3,0:T(8,128)}, u32[]{:S(2)}) copy-start(f32[1,2,128,2,512]{4,2,1,3,0:T(8,128)} %copy.144) | copy-start | bytes 3145732
Sparse Core Ops, SparseCore 0:
  379.9 62.2 reduce-scatter.3
where the time goes:
time: 456 us; the launch traced here: 451 us
  matrix products  237 us (52%)
  waiting for transfers between devices  134 us (29%)
  local copies, waits for them, and re-layouts  44.7 us (10%)
  between operations  14.8 us (3%)
  other arithmetic  11.5 us (3%)
  starting transfers between devices  9.48 us (2%)
    dot_general x28, matrix products, along_rows(): jnp.einsum('kn,fnj->fkj', matrix, values, precision=lax.Precision.HIGHEST...  164 us
    dot_general x8, matrix products, along_last(): jnp.einsum('...n,nk->...k', values, matrix, precision=lax.Precision.HIGHE...  72.2 us
    all_to_all x1, waiting for transfers between devices, on_device(): lax.all_to_all(jnp.stack(shifted_all, axis=1), 'pencil', split_axis=2, co...  63.3 us
    unnamed x2, waiting for transfers between devices  60.6 us
    all_to_all x2, local copies, waits for them, and re-layouts, on_device(): lax.all_to_all(jnp.stack(shifted_all, axis=1), 'pencil', split_axis=2, co...  17.7 us
    another operation x1, local copies, waits for them, and re-layouts, on_device(): jnp.stack(shifted_all, axis=1)  10.3 us
    all_to_all x1, waiting for transfers between devices, on_device(): lax.all_to_all(jnp.stack([spec_real, spec_imag], axis=2), 'pencil', split...  9.89 us
  transfers between devices with their start and end apart: 3, of which 3 were waited for; matrix products, arithmetic and copies ran while one was open for 3% of the time, Pallas kernels for 0%

commit v1 on v0

v1 whole, which is shorter than its diff:
```python
import functools
import math

import jax
import jax.numpy as jnp
import ml_dtypes
import numpy as np
from jax import lax
from jax.experimental import pallas as pl
from jax.experimental.pallas import tpu as pltpu
from jax.sharding import PartitionSpec as P

GRID_SPACING = 12.5
DEPTH_STEP = 10.0
MESH = pl.DeviceIdType.MESH


def real_tables(length):
    half, quarter = length // 2, length // 4
    points = np.arange(half)
    out = []
    for parity in (0, 1):
        waves = 2 * np.arange(quarter) + parity
        angles = 2.0 * np.pi * ((waves[:, None] * points[None, :]) % length) / length
        cosines = np.cos(angles) * math.sqrt(2.0 / length)
        sines = np.sin(angles) * math.sqrt(2.0 / length)
        if parity == 0:
            cosines[0] = 1.0 / math.sqrt(length)
            sines[0] = np.where(points % 2 == 0, 1.0, -1.0) / math.sqrt(length)
        out.append(np.concatenate([cosines, sines]))
    table = np.stack(out)
    both = np.stack([table, table.transpose(0, 2, 1)])
    high = both.astype(ml_dtypes.bfloat16)
    low = (both - high.astype(np.float64)).astype(ml_dtypes.bfloat16)
    return high, low


def halves(values):
    high = values.astype(jnp.bfloat16)
    low = (values - high.astype(jnp.float32)).astype(jnp.bfloat16)
    return high, low


def dot(a, b):
    return jnp.dot(a, b, preferred_element_type=jnp.float32)


def product(a, b):
    return dot(a[0], b[0]) + (dot(a[0], b[1]) + dot(a[1], b[0]))


def kernel(
    dims,
    wave_ref,
    source_ref,
    high_x,
    low_x,
    high_y,
    low_y,
    omega_ref,
    speed_ref,
    lower_ref,
    weight_ref,
    out_ref,
    image_ref,
    stage,
    recv,
    phase,
    shifted,
    coef,
    blend_own,
    blend_recv,
    img_send,
    img_recv,
    send_sem,
    recv_sem,
    pair_send,
    pair_recv,
    isend_sem,
    irecv_sem,
):
    freqs, pencils, groups, rows, width_x, width_y, refs, tile, scale = dims
    chips = pencils // 2
    half_x, half_y = width_x // 2, width_y // 2
    quarter_x, quarter_y = width_x // 4, width_y // 4
    band = 2 * rows
    me = lax.axis_index("pencil")
    group = lax.axis_index("freq")
    core = lax.rem(me, 2)
    chip = lax.div(me, 2)
    partner = chip * 2 + (1 - core)

    barrier = pltpu.get_barrier_semaphore()
    for step in range(1, pencils):
        pl.semaphore_signal(
            barrier, inc=1, device_id=(group, lax.rem(me + step, pencils)), device_id_type=MESH
        )
    for step in range(1, groups):
        pl.semaphore_signal(
            barrier, inc=1, device_id=(lax.rem(group + step, groups), me), device_id_type=MESH
        )

    sends = []
    for f in range(freqs):
        for c in range(2):
            values = wave_ref[f, c]
            first, second = values[:, :half_y], values[:, half_y:]
            for e in range(2):
                mixed = first + second if e == 0 else first - second
                stage[f, e, c] = product(halves(mixed), (high_y[1, e], low_y[1, e]))
        recv[f, me] = stage[f, core]
        if f == 0:
            pl.semaphore_wait(barrier, pencils - 1 + groups - 1)
        for far in list(range(1, chips)) + [0]:
            for flip in range(2):
                if far == 0 and flip == 0:
                    continue
                to_core = (core + flip) % 2
                slot = far * 2 + flip
                target = lax.rem(chip + far, chips) * 2 + to_core
                copy = pltpu.make_async_remote_copy(
                    src_ref=stage.at[f, to_core],
                    dst_ref=recv.at[f, me],
                    send_sem=send_sem.at[f, slot],
                    recv_sem=recv_sem.at[f, slot],
                    device_id=(group, target),
                    device_id_type=MESH,
                )
                copy.start()
                sends.append((f, copy))

    tile_rows = band // tile
    tiles_y = width_y // tile
    lane_y = lax.broadcasted_iota(jnp.int32, (8, width_y), 1)
    bases = []
    for t in range(tile_rows):
        row = chip * tile_rows + t
        lowers = [lower_ref[row, q] for q in range(tiles_y)]
        base = functools.reduce(jnp.minimum, lowers)
        base = jnp.minimum(base, refs - 3)
        bases.append(base)
        for k in range(3):
            line = jnp.zeros((8, width_y), jnp.float32)
            for q in range(tiles_y):
                w = weight_ref[row, q]
                value = jnp.where(lowers[q] == base + k, w, 0.0) + jnp.where(
                    lowers[q] + 1 == base + k, 1.0 - w, 0.0
                )
                line = jnp.where((lane_y >= q * tile) & (lane_y < (q + 1) * tile), value, line)
            coef[t, k] = line

    step_x = 2.0 * math.pi / (width_x * GRID_SPACING)
    step_y = 2.0 * math.pi / (width_y * GRID_SPACING)

    def terms(angular, velocity, radial):
        vertical = (angular / velocity) ** 2 - radial
        travel = jnp.sqrt(jnp.maximum(vertical, 0.0)) * DEPTH_STEP
        damping = jnp.exp(-jnp.sqrt(jnp.maximum(-vertical, 0.0)) * DEPTH_STEP)
        return damping * jnp.cos(travel), damping * jnp.sin(travel)

    lanes = lax.broadcasted_iota(jnp.int32, (1, quarter_y), 1)
    ky = (2 * lanes + core).astype(jnp.float32) * step_y
    ky_extra = jnp.where(core == 0, half_y, 1).astype(jnp.float32) * step_y
    even_rows = 2 * lax.broadcasted_iota(jnp.int32, (quarter_x, 1), 0)
    kx_even = even_rows.astype(jnp.float32) * step_x
    kx_odd = (even_rows + 1).astype(jnp.float32) * step_x
    kx_last = jnp.full((8, 1), half_x, jnp.int32).astype(jnp.float32) * step_x
    row_id = lax.broadcasted_iota(jnp.int32, (quarter_x, quarter_y), 0)
    lane_id = lax.broadcasted_iota(jnp.int32, (quarter_x, quarter_y), 1)
    speeds_row = jnp.full((1, quarter_y), speed_ref[0, 0], jnp.float32)
    for r in range(1, refs):
        speeds_row = jnp.where(lanes == r, speed_ref[0, r], speeds_row)

    for f in range(freqs):
        angular = omega_ref[f]
        extra = [
            terms(angular, speeds_row, kx * kx + ky_extra * ky_extra)
            for kx in (kx_even, kx_last, kx_odd)
        ]
        for r in range(refs):
            velocity = speed_ref[0, r]
            main = [
                terms(angular, velocity, kx * kx + ky * ky) for kx in (kx_even, kx_last, kx_odd)
            ]
            for part in range(2):
                even, last, odd = (m[part] for m in main)
                even_x, last_x, odd_x = (m[part][:, r : r + 1] for m in extra)
                even_s = jnp.where(row_id == 0, last[0:1], even)
                even_sx = jnp.where(row_id[:, 0:1] == 0, last_x[0:1], even_x)
                blocks = ((even, even_x), (even_s, even_sx), (odd, odd_x), (odd, odd_x))
                for i, (block, column) in enumerate(blocks):
                    span = slice(i * quarter_x, (i + 1) * quarter_x)
                    phase[f, r, part, span, :quarter_y] = block
                    phase[f, r, part, span, quarter_y:] = jnp.where(lane_id == 0, column, block)

    start = lax.rem(chip * band, half_x)
    sign_x = jnp.where(chip * band < half_x, 1.0, -1.0)
    sign_y = jnp.where(core == 0, 1.0, -1.0)
    start = pl.multiple_of(start, rows)
    back = [
        (high_x[1, e, pl.ds(start, band), :], low_x[1, e, pl.ds(start, band), :]) for e in range(2)
    ]
    table_y = (high_y[0, core], low_y[0, core])

    pair_copies = []
    for f in range(freqs):
        for g, copy in sends:
            if g == f:
                copy.wait_recv()
        spectrum = []
        for c in range(2):
            upper = recv[f, 0 : pencils // 2, c].reshape(half_x, half_y)
            lower = recv[f, pencils // 2 : pencils, c].reshape(half_x, half_y)
            even = product((high_x[0, 0], low_x[0, 0]), halves(upper + lower))
            odd = product((high_x[0, 1], low_x[0, 1]), halves(upper - lower))
            spectrum.append((even, odd))

        def one_ref(r, carry):
            total = [None, None]
            for e in range(2):
                span = slice(e * half_x, (e + 1) * half_x)
                real, imag = spectrum[0][e], spectrum[1][e]
                pc, ps = phase[f, r, 0, span, :], phase[f, r, 1, span, :]
                moved = (real * pc - imag * ps, real * ps + imag * pc)
                for c in range(2):
                    share = product(back[e], halves(moved[c]))
                    total[c] = share if e == 0 else total[c] + sign_x * share
            for c in range(2):
                shifted[r, c] = total[c]
            return carry

        for r in range(refs):
            one_ref(r, 0)

        for t in range(tile_rows):
            lo, hi = [None, None], [None, None]
            for k in range(3):
                block = shifted[bases[t] + k, :, t * tile : (t + 1) * tile, :]
                space = product(halves(block.reshape(2 * tile, half_y)), table_y)
                for c in range(2):
                    piece = space[c * tile : (c + 1) * tile]
                    a = coef[t, k, 0:1, :half_y] * piece
                    b = coef[t, k, 0:1, half_y:] * piece
                    lo[c] = a if k == 0 else lo[c] + a
                    hi[c] = b if k == 0 else hi[c] + b
            owner, inner = (t * tile) // rows, (t * tile) % rows
            for c in range(2):
                blend_own[f, owner, c, inner : inner + tile, :half_y] = lo[c]
                blend_own[f, owner, c, inner : inner + tile, half_y:] = hi[c] * sign_y
        copy = pltpu.make_async_remote_copy(
            src_ref=blend_own.at[f, 1 - core],
            dst_ref=blend_recv.at[f],
            send_sem=pair_send.at[f],
            recv_sem=pair_recv.at[f],
            device_id=(group, partner),
            device_id_type=MESH,
        )
        copy.start()
        pair_copies.append(copy)

    image = None
    for f in range(freqs):
        pair_copies[f].wait_recv()
        for c in range(2):
            value = blend_own[f, core, c] + blend_recv[f, c]
            out_ref[f, c] = value
            term = source_ref[f, c] * value
            image = term if image is None else image + term
    image = image * scale

    own_width = width_y // groups
    packs = 128 // own_width
    chunk = rows // packs
    lane = lax.broadcasted_iota(jnp.int32, (chunk, 128), 1)
    for g in range(groups):
        at = g * own_width
        column = image[:, at // 128 * 128 : at // 128 * 128 + 128]
        offset = at % 128
        packed = None
        for i in range(packs):
            part = column[i * chunk : (i + 1) * chunk]
            shift = (i * own_width - offset) % 128
            if shift:
                part = pltpu.roll(part, shift, 1)
            packed = part if packed is None else jnp.where(lane >= i * own_width, part, packed)
        img_send[g] = packed
    image_copies = []
    for step in range(1, groups):
        to = lax.rem(group + step, groups)
        copy = pltpu.make_async_remote_copy(
            src_ref=img_send.at[to],
            dst_ref=img_recv.at[step],
            send_sem=isend_sem.at[step],
            recv_sem=irecv_sem.at[step],
            device_id=(to, me),
            device_id_type=MESH,
        )
        copy.start()
        image_copies.append(copy)
    total = img_send[group]
    for step, copy in enumerate(image_copies):
        copy.wait_recv()
        total = total + img_recv[step + 1]
    for i in range(packs):
        part = pltpu.roll(total, (-i * own_width) % 128, 1) if i else total
        image_ref[i * chunk : (i + 1) * chunk, :] = part[:, :own_width]

    for _, copy in sends:
        copy.wait_send()
    for copy in pair_copies:
        copy.wait_send()
    for copy in image_copies:
        copy.wait_send()


def on_device(wave_field, source_field, omegas, velocities, lower_ref, blend_weight):
    pencils = lax.axis_size("pencil")
    groups = lax.axis_size("freq")
    freqs, rows, _, width_y = wave_field.shape
    width_x = rows * pencils
    refs = velocities.shape[1]
    tile = width_x // lower_ref.shape[1]
    half_y = width_y // 2
    scale = 1.0 / math.sqrt(freqs * groups)
    dims = (freqs, pencils, groups, rows, width_x, width_y, refs, tile, scale)
    own_width = width_y // groups
    tables = [jnp.asarray(t) for t in real_tables(width_x) + real_tables(width_y)]
    wave = jnp.transpose(wave_field, (0, 2, 1, 3))
    source = jnp.transpose(source_field[0], (0, 2, 1, 3))
    vmem = pl.BlockSpec(memory_space=pltpu.VMEM)
    smem = pl.BlockSpec(memory_space=pltpu.SMEM)
    f32 = jnp.float32
    packed = (groups, rows * own_width // 128, 128)
    out, image = pl.pallas_call(
        functools.partial(kernel, dims),
        out_shape=(
            jax.ShapeDtypeStruct((freqs, 2, rows, width_y), f32),
            jax.ShapeDtypeStruct((rows, own_width), f32),
        ),
        in_specs=[vmem] * 6 + [smem] * 4,
        out_specs=(vmem, vmem),
        scratch_shapes=[
            pltpu.VMEM((freqs, 2, 2, rows, half_y), f32),
            pltpu.VMEM((freqs, pencils, 2, rows, half_y), f32),
            pltpu.VMEM((freqs, refs, 2, width_x, half_y), f32),
            pltpu.VMEM((refs, 2, 2 * rows, half_y), f32),
            pltpu.VMEM((2 * rows // tile, 3, 8, width_y), f32),
            pltpu.VMEM((freqs, 2, 2, rows, width_y), f32),
            pltpu.VMEM((freqs, 2, rows, width_y), f32),
            pltpu.VMEM(packed, f32),
            pltpu.VMEM(packed, f32),
            pltpu.SemaphoreType.DMA((freqs, pencils)),
            pltpu.SemaphoreType.DMA((freqs, pencils)),
            pltpu.SemaphoreType.DMA((freqs,)),
            pltpu.SemaphoreType.DMA((freqs,)),
            pltpu.SemaphoreType.DMA((groups,)),
            pltpu.SemaphoreType.DMA((groups,)),
        ],
        compiler_params=pltpu.CompilerParams(
            collective_id=0, has_side_effects=True, vmem_limit_bytes=56 * 1024 * 1024
        ),
    )(wave, source, *tables, omegas, velocities, lower_ref[0], blend_weight[0])
    return jnp.transpose(out, (0, 2, 1, 3)), image[None]


def solution(mesh):
    placed = (
        P("freq", "pencil", None, None),
        P(None, "freq", "pencil", None, None),
        P("freq"),
        P(),
        P(),
        P(),
    )
    return jax.shard_map(
        on_device,
        mesh=mesh,
        in_specs=placed,
        out_specs=(P("freq", "pencil", None, None), P(None, "pencil", "freq")),
        check_vma=False,
    )
```

time: 456 us -> 54 us (0.12); the launches traced: 451 us -> 53.8 us
  matrix products: 237 us -> 0 us
  waiting for transfers between devices: 134 us -> 0 us
  Pallas kernels: 0 us -> 45.7 us
  local copies, waits for them, and re-layouts: 44.7 us -> 7.4 us
  between operations: 14.8 us -> 0.66 us
  other arithmetic: 11.5 us -> 0 us
  starting transfers between devices: 9.48 us -> 0 us
    dot_general x36 -> x0, matrix products: 237 us -> none  [the longest x28 164 us: along_rows(): jnp.einsum('kn,fnj->fkj', matrix, values, precision=lax.Precision.HIGHEST...]
    all_to_all x2 -> x0, waiting for transfers between devices: 73.2 us -> none  [the longest x1 63.3 us: on_device(): lax.all_to_all(jnp.stack(shifted_all, axis=1), 'pencil', split_axis=2, co...]
    unnamed x2 -> x0, waiting for transfers between devices: 60.6 us -> none
    pallas_call x0 -> x1, Pallas kernels: none -> 45.7 us  [on_device(): pl.pallas_call(functools.partial(kernel, dims), out_shape=(jax.ShapeDtype...]
    all_to_all x4 -> x0, local copies, waits for them, and re-layouts: 18.8 us -> none  [the longest x2 17.7 us: on_device(): lax.all_to_all(jnp.stack(shifted_all, axis=1), 'pencil', split_axis=2, co...]
    another operation x4 -> x0, local copies, waits for them, and re-layouts: 12.6 us -> none  [the longest x1 10.3 us: on_device(): jnp.stack(shifted_all, axis=1)]
    all_to_all x2 -> x0, starting transfers between devices: 9.44 us -> none  [the longest x1 5.23 us: on_device(): lax.all_to_all(jnp.stack(shifted_all, axis=1), 'pencil', split_axis=2, co...]
    unnamed x5 -> x0, other arithmetic: 5.28 us -> none
  transfers between devices with their start and end apart: 3 -> 0, of which waited for: 3 -> 0; matrix products, arithmetic and copies ran while one was open for 3% -> 0% of each run, Pallas kernels for 0% -> 0%
where the time goes in v1:
time: 54 us; the launch traced here: 53.8 us
  Pallas kernels  45.7 us (85%)
  local copies, waits for them, and re-layouts  7.4 us (14%)
  between operations  0.66 us (1%)
    pallas_call x1, Pallas kernels, on_device(): pl.pallas_call(functools.partial(kernel, dims), out_shape=(jax.ShapeDtype...  45.7 us
    unnamed x8, local copies, waits for them, and re-layouts  7.4 us

profile of v1, /device:TPU:0, one launch (start us, length us, event | category | flops | bytes accessed | tf_op | source)
XLA Modules:
  0.0 53.8 jit_solution(365414721768188454)
XLA Ops:
  0.6 0.0 copy-start
  0.6 2.5 %copy.19 = f32[2,128,2,512]{3,1,2,0:T(8,128)} copy(f32[2,128,2,512]{3,2,1,0:T(2,128)} %param.10) | data formatting | bytes 2097152 | tf_op args[0]
  3.1 0.0 copy-done
  3.1 1.2 %copy.18 = f32[1,2,128,2,512]{4,2,3,1,0:T(8,128)} copy(f32[1,2,128,2,512]{4,3,2,1,0:T(2,128)S(1)} %copy-done) | data formatting | bytes 2097152 | tf_op args[1]
  4.3 45.7 %shard_map.113 = (f32[2,2,128,512]{3,2,1,0:T(8,128)}, f32[128,64]{1,0:T(8,128)}) custom-call(f32[2,2,128,512]{3,2,1,0:T(8,128)} %bitcast.12, f32[2,2,128,512]{3,2,1,0:T(8,128)} %bitcast.13, bf16[2,2,256,256]{3,2,1,0:T(8,128)(2,1)} %constant.4.clone.high_x.high_y, bf16[2,2,256,256]{3,2,1,0:T(8,128)(2,1)} %constant.5.clone.low_x.low_y, ...), custom_call_target="tpu_custom_call" | custom-call | tf_op jit(solution)/shard_map/pallas_call | solution.py:334
  50.0 0.0 copy-start.1
  50.1 3.0 %copy.14 = f32[2,128,2,512]{3,2,1,0:T(2,128)} copy(f32[2,128,2,512]{3,1,2,0:T(8,128)} %bitcast.14) | data formatting | bytes 2097152
  53.1 0.0 copy-done.1
  53.1 0.7 %copy.15 = f32[1,128,64]{1,2,0:T(8,128)} copy(f32[1,128,64]{2,1,0:T(8,128)S(1)} %bitcast.15) | data formatting | bytes 65536
Async XLA Ops:
  0.6 2.5 %copy-start = (f32[1,2,128,2,512]{4,3,2,1,0:T(2,128)S(1)}, f32[1,2,128,2,512]{4,3,2,1,0:T(2,128)}, u32[]{:S(2)}) copy-start(f32[1,2,128,2,512]{4,3,2,1,0:T(2,128)} %param.11) | copy-start | bytes 3145732
  50.0 3.0 %copy-start.1 = (f32[128,64]{1,0:T(8,128)S(1)}, f32[128,64]{1,0:T(8,128)}, u32[]{:S(2)}) copy-start(f32[128,64]{1,0:T(8,128)} %get-tuple-element.5) | copy-start | bytes 98308

commit v2 on v1

--- a/solution.py
+++ b/solution.py
@@ -53,10 +53,12 @@
     dims,
     wave_ref,
     source_ref,
-    high_x,
-    low_x,
-    high_y,
-    low_y,
+    high_fwd,
+    low_fwd,
+    high_x_ref,
+    low_x_ref,
+    high_back_ref,
+    low_back_ref,
     omega_ref,
     speed_ref,
     lower_ref,
@@ -69,9 +71,21 @@
     shifted,
     coef,
     blend_own,
+    blend_send,
     blend_recv,
+    img_acc,
     img_send,
     img_recv,
+    wave_buf,
+    source_buf,
+    out_buf,
+    high_x,
+    low_x,
+    high_back,
+    low_back,
+    table_sem,
+    load_sem,
+    store_sem,
     send_sem,
     recv_sem,
     pair_send,
@@ -90,6 +104,24 @@
     chip = lax.div(me, 2)
     partner = chip * 2 + (1 - core)
 
+    per = rows // tile
+    loads = {}
+    for kind, (ref, buf) in enumerate(((wave_ref, wave_buf), (source_ref, source_buf))):
+        for f in range(freqs):
+            for c in range(2):
+                src = ref.at[f, :, c, :] if kind == 0 else ref.at[0, f, :, c, :]
+                copy = pltpu.make_async_copy(src, buf.at[f, c], load_sem.at[kind, f, c])
+                copy.start()
+                loads[kind, f, c] = copy
+
+    tables = []
+    for i, (ref, buf) in enumerate(
+        ((high_x_ref, high_x), (low_x_ref, low_x), (high_back_ref, high_back), (low_back_ref, low_back))
+    ):
+        copy = pltpu.make_async_copy(ref, buf, table_sem.at[i])
+        copy.start()
+        tables.append(copy)
+
     barrier = pltpu.get_barrier_semaphore()
     for step in range(1, pencils):
         pl.semaphore_signal(
@@ -103,38 +135,43 @@
     sends = []
     for f in range(freqs):
         for c in range(2):
-            values = wave_ref[f, c]
+            loads[0, f, c].wait()
+            values = wave_buf[f, c]
             first, second = values[:, :half_y], values[:, half_y:]
-            for e in range(2):
-                mixed = first + second if e == 0 else first - second
-                stage[f, e, c] = product(halves(mixed), (high_y[1, e], low_y[1, e]))
-        recv[f, me] = stage[f, core]
-        if f == 0:
-            pl.semaphore_wait(barrier, pencils - 1 + groups - 1)
-        for far in list(range(1, chips)) + [0]:
-            for flip in range(2):
-                if far == 0 and flip == 0:
-                    continue
-                to_core = (core + flip) % 2
-                slot = far * 2 + flip
-                target = lax.rem(chip + far, chips) * 2 + to_core
-                copy = pltpu.make_async_remote_copy(
-                    src_ref=stage.at[f, to_core],
-                    dst_ref=recv.at[f, me],
-                    send_sem=send_sem.at[f, slot],
-                    recv_sem=recv_sem.at[f, slot],
-                    device_id=(group, target),
-                    device_id_type=MESH,
-                )
-                copy.start()
-                sends.append((f, copy))
+            for flip in (1, 0):
+                to_core = lax.rem(core + flip, 2)
+                sign = jnp.where(to_core == 0, 1.0, -1.0)
+                mixed = halves(first + sign * second)
+                piece = product(mixed, (high_fwd[to_core], low_fwd[to_core]))
+                stage[f, c, flip] = piece
+                if flip == 0:
+                    recv[f, me, c] = piece
+                if f == 0 and c == 0 and flip == 1:
+                    pl.semaphore_wait(barrier, pencils - 1 + groups - 1)
+                for far in list(range(1, chips)) + [0]:
+                    if far == 0 and flip == 0:
+                        continue
+                    slot = far * 2 + flip
+                    target = lax.rem(chip + far, chips) * 2 + to_core
+                    copy = pltpu.make_async_remote_copy(
+                        src_ref=stage.at[f, c, flip],
+                        dst_ref=recv.at[f, me, c],
+                        send_sem=send_sem.at[f, c, slot],
+                        recv_sem=recv_sem.at[f, c, slot],
+                        device_id=(group, target),
+                        device_id_type=MESH,
+                    )
+                    copy.start()
+                    sends.append((f, c, copy))
 
     tile_rows = band // tile
     tiles_y = width_y // tile
     lane_y = lax.broadcasted_iota(jnp.int32, (8, width_y), 1)
-    bases = []
+    bases, offsets = [], []
     for t in range(tile_rows):
-        row = chip * tile_rows + t
+        owner = 1 - core if t < per else core
+        row = chip * tile_rows + owner * per + t % per
+        offsets.append(pl.multiple_of(owner * rows + (t % per) * tile, tile))
         lowers = [lower_ref[row, q] for q in range(tiles_y)]
         base = functools.reduce(jnp.minimum, lowers)
         base = jnp.minimum(base, refs - 3)
@@ -193,6 +230,8 @@
                     phase[f, r, part, span, :quarter_y] = block
                     phase[f, r, part, span, quarter_y:] = jnp.where(lane_id == 0, column, block)
 
+    for copy in tables:
+        copy.wait()
     start = lax.rem(chip * band, half_x)
     sign_x = jnp.where(chip * band < half_x, 1.0, -1.0)
     sign_y = jnp.where(core == 0, 1.0, -1.0)
@@ -200,15 +239,69 @@
     back = [
         (high_x[1, e, pl.ds(start, band), :], low_x[1, e, pl.ds(start, band), :]) for e in range(2)
     ]
-    table_y = (high_y[0, core], low_y[0, core])
-
-    pair_copies = []
+    table_y = (high_back[core], low_back[core])
+
+    own_width = width_y // groups
+    packs = 128 // own_width
+    chunk = tile // packs
+    lane = lax.broadcasted_iota(jnp.int32, (chunk, 128), 1)
+    pair_copies, stores, image_copies = [], [], []
+
+    def finish(f):
+        last = f == freqs - 1
+        for i in range(per):
+            span = slice(i * tile, (i + 1) * tile)
+            pair_copies[f * per + i].wait_recv()
+            image = None
+            for c in range(2):
+                value = blend_own[f, c, span] + blend_recv[f, i, c]
+                out_buf[f, c, span] = value
+                if i == 0:
+                    loads[1, f, c].wait()
+                term = source_buf[f, c, span] * value
+                image = term if image is None else image + term
+            if f > 0:
+                image = image + img_acc[span]
+            if not last:
+                img_acc[span] = image
+                continue
+            image = image * scale
+            for g in range(groups):
+                at = g * own_width
+                column = image[:, at // 128 * 128 : at // 128 * 128 + 128]
+                packed = None
+                for j in range(packs):
+                    part = column[j * chunk : (j + 1) * chunk]
+                    shift = (j * own_width - at) % 128
+                    if shift:
+                        part = pltpu.roll(part, shift, 1)
+                    packed = part if packed is None else jnp.where(lane >= j * own_width, part, packed)
+                img_send[i, g] = packed
+            for step in range(1, groups):
+                to = lax.rem(group + step, groups)
+                copy = pltpu.make_async_remote_copy(
+                    src_ref=img_send.at[i, to],
+                    dst_ref=img_recv.at[i, step],
+                    send_sem=isend_sem.at[i, step],
+                    recv_sem=irecv_sem.at[i, step],
+                    device_id=(to, me),
+                    device_id_type=MESH,
+                )
+                copy.start()
+                image_copies.append((i, step, copy))
+        for c in range(2):
+            copy = pltpu.make_async_copy(out_buf.at[f, c], out_ref.at[f, :, c, :], store_sem.at[f, c])
+            copy.start()
+            stores.append(copy)
+
     for f in range(freqs):
-        for g, copy in sends:
-            if g == f:
-                copy.wait_recv()
+        if f > 0:
+            finish(f - 1)
         spectrum = []
         for c in range(2):
+            for g, d, copy in sends:
+                if (g, d) == (f, c):
+                    copy.wait_recv()
             upper = recv[f, 0 : pencils // 2, c].reshape(half_x, half_y)
             lower = recv[f, pencils // 2 : pencils, c].reshape(half_x, half_y)
             even = product((high_x[0, 0], low_x[0, 0]), halves(upper + lower))
@@ -235,7 +328,7 @@
         for t in range(tile_rows):
             lo, hi = [None, None], [None, None]
             for k in range(3):
-                block = shifted[bases[t] + k, :, t * tile : (t + 1) * tile, :]
+                block = shifted[bases[t] + k, :, pl.ds(offsets[t], tile), :]
                 space = product(halves(block.reshape(2 * tile, half_y)), table_y)
                 for c in range(2):
                     piece = space[c * tile : (c + 1) * tile]
@@ -243,73 +336,46 @@
                     b = coef[t, k, 0:1, half_y:] * piece
                     lo[c] = a if k == 0 else lo[c] + a
                     hi[c] = b if k == 0 else hi[c] + b
-            owner, inner = (t * tile) // rows, (t * tile) % rows
+            inner = (t % per) * tile
             for c in range(2):
-                blend_own[f, owner, c, inner : inner + tile, :half_y] = lo[c]
-                blend_own[f, owner, c, inner : inner + tile, half_y:] = hi[c] * sign_y
-        copy = pltpu.make_async_remote_copy(
-            src_ref=blend_own.at[f, 1 - core],
-            dst_ref=blend_recv.at[f],
-            send_sem=pair_send.at[f],
-            recv_sem=pair_recv.at[f],
-            device_id=(group, partner),
-            device_id_type=MESH,
-        )
-        copy.start()
-        pair_copies.append(copy)
-
-    image = None
-    for f in range(freqs):
-        pair_copies[f].wait_recv()
-        for c in range(2):
-            value = blend_own[f, core, c] + blend_recv[f, c]
-            out_ref[f, c] = value
-            term = source_ref[f, c] * value
-            image = term if image is None else image + term
-    image = image * scale
-
-    own_width = width_y // groups
-    packs = 128 // own_width
-    chunk = rows // packs
-    lane = lax.broadcasted_iota(jnp.int32, (chunk, 128), 1)
-    for g in range(groups):
-        at = g * own_width
-        column = image[:, at // 128 * 128 : at // 128 * 128 + 128]
-        offset = at % 128
-        packed = None
-        for i in range(packs):
-            part = column[i * chunk : (i + 1) * chunk]
-            shift = (i * own_width - offset) % 128
-            if shift:
-                part = pltpu.roll(part, shift, 1)
-            packed = part if packed is None else jnp.where(lane >= i * own_width, part, packed)
-        img_send[g] = packed
-    image_copies = []
-    for step in range(1, groups):
-        to = lax.rem(group + step, groups)
-        copy = pltpu.make_async_remote_copy(
-            src_ref=img_send.at[to],
-            dst_ref=img_recv.at[step],
-            send_sem=isend_sem.at[step],
-            recv_sem=irecv_sem.at[step],
-            device_id=(to, me),
-            device_id_type=MESH,
-        )
-        copy.start()
-        image_copies.append(copy)
-    total = img_send[group]
-    for step, copy in enumerate(image_copies):
-        copy.wait_recv()
-        total = total + img_recv[step + 1]
-    for i in range(packs):
-        part = pltpu.roll(total, (-i * own_width) % 128, 1) if i else total
-        image_ref[i * chunk : (i + 1) * chunk, :] = part[:, :own_width]
-
-    for _, copy in sends:
+                if t < per:
+                    blend_send[f, t, c, :, :half_y] = lo[c]
+                    blend_send[f, t, c, :, half_y:] = hi[c] * sign_y
+                else:
+                    blend_own[f, c, inner : inner + tile, :half_y] = lo[c]
+                    blend_own[f, c, inner : inner + tile, half_y:] = hi[c] * sign_y
+            if t < per:
+                copy = pltpu.make_async_remote_copy(
+                    src_ref=blend_send.at[f, t],
+                    dst_ref=blend_recv.at[f, t],
+                    send_sem=pair_send.at[f, t],
+                    recv_sem=pair_recv.at[f, t],
+                    device_id=(group, partner),
+                    device_id_type=MESH,
+                )
+                copy.start()
+                pair_copies.append(copy)
+    finish(freqs - 1)
+
+    lines = []
+    for i in range(per):
+        total = img_send[i, group]
+        for j, step, copy in image_copies:
+            if j == i:
+                copy.wait_recv()
+                total = total + img_recv[i, step]
+        for j in range(packs):
+            part = pltpu.roll(total, (-j * own_width) % 128, 1) if j else total
+            lines.append(part[:, :own_width])
+    image_ref[...] = jnp.concatenate(lines, axis=0).T
+
+    for copy in stores:
+        copy.wait()
+    for _, _, copy in sends:
         copy.wait_send()
     for copy in pair_copies:
         copy.wait_send()
-    for copy in image_copies:
+    for _, _, copy in image_copies:
         copy.wait_send()
 
 
@@ -324,43 +390,57 @@
     scale = 1.0 / math.sqrt(freqs * groups)
     dims = (freqs, pencils, groups, rows, width_x, width_y, refs, tile, scale)
     own_width = width_y // groups
-    tables = [jnp.asarray(t) for t in real_tables(width_x) + real_tables(width_y)]
-    wave = jnp.transpose(wave_field, (0, 2, 1, 3))
-    source = jnp.transpose(source_field[0], (0, 2, 1, 3))
+    high_x, low_x = real_tables(width_x)
+    high_y, low_y = real_tables(width_y)
+    tables = [jnp.asarray(t) for t in (high_y[1], low_y[1], high_x, low_x, high_y[0], low_y[0])]
+    hbm = pl.BlockSpec(memory_space=pl.ANY)
     vmem = pl.BlockSpec(memory_space=pltpu.VMEM)
     smem = pl.BlockSpec(memory_space=pltpu.SMEM)
     f32 = jnp.float32
-    packed = (groups, rows * own_width // 128, 128)
+    per = rows // tile
+    packed = (per, groups, tile * own_width // 128, 128)
     out, image = pl.pallas_call(
         functools.partial(kernel, dims),
         out_shape=(
-            jax.ShapeDtypeStruct((freqs, 2, rows, width_y), f32),
-            jax.ShapeDtypeStruct((rows, own_width), f32),
+            jax.ShapeDtypeStruct(wave_field.shape, f32),
+            jax.ShapeDtypeStruct((own_width, rows), f32),
         ),
-        in_specs=[vmem] * 6 + [smem] * 4,
-        out_specs=(vmem, vmem),
+        in_specs=[hbm] * 2 + [vmem] * 2 + [hbm] * 4 + [smem] * 4,
+        out_specs=(hbm, vmem),
         scratch_shapes=[
             pltpu.VMEM((freqs, 2, 2, rows, half_y), f32),
             pltpu.VMEM((freqs, pencils, 2, rows, half_y), f32),
             pltpu.VMEM((freqs, refs, 2, width_x, half_y), f32),
             pltpu.VMEM((refs, 2, 2 * rows, half_y), f32),
-            pltpu.VMEM((2 * rows // tile, 3, 8, width_y), f32),
-            pltpu.VMEM((freqs, 2, 2, rows, width_y), f32),
+            pltpu.VMEM((2 * per, 3, 8, width_y), f32),
             pltpu.VMEM((freqs, 2, rows, width_y), f32),
+            pltpu.VMEM((freqs, per, 2, tile, width_y), f32),
+            pltpu.VMEM((freqs, per, 2, tile, width_y), f32),
+            pltpu.VMEM((rows, width_y), f32),
             pltpu.VMEM(packed, f32),
             pltpu.VMEM(packed, f32),
-            pltpu.SemaphoreType.DMA((freqs, pencils)),
-            pltpu.SemaphoreType.DMA((freqs, pencils)),
-            pltpu.SemaphoreType.DMA((freqs,)),
-            pltpu.SemaphoreType.DMA((freqs,)),
-            pltpu.SemaphoreType.DMA((groups,)),
-            pltpu.SemaphoreType.DMA((groups,)),
+            pltpu.VMEM((freqs, 2, rows, width_y), f32),
+            pltpu.VMEM((freqs, 2, rows, width_y), f32),
+            pltpu.VMEM((freqs, 2, rows, width_y), f32),
+            pltpu.VMEM(high_x.shape, jnp.bfloat16),
+            pltpu.VMEM(high_x.shape, jnp.bfloat16),
+            pltpu.VMEM(high_y.shape[1:], jnp.bfloat16),
+            pltpu.VMEM(high_y.shape[1:], jnp.bfloat16),
+            pltpu.SemaphoreType.DMA((4,)),
+            pltpu.SemaphoreType.DMA((2, freqs, 2)),
+            pltpu.SemaphoreType.DMA((freqs, 2)),
+            pltpu.SemaphoreType.DMA((freqs, 2, pencils)),
+            pltpu.SemaphoreType.DMA((freqs, 2, pencils)),
+            pltpu.SemaphoreType.DMA((freqs, per)),
+            pltpu.SemaphoreType.DMA((freqs, per)),
+            pltpu.SemaphoreType.DMA((per, groups)),
+            pltpu.SemaphoreType.DMA((per, groups)),
         ],
         compiler_params=pltpu.CompilerParams(
             collective_id=0, has_side_effects=True, vmem_limit_bytes=56 * 1024 * 1024
         ),
-    )(wave, source, *tables, omegas, velocities, lower_ref[0], blend_weight[0])
-    return jnp.transpose(out, (0, 2, 1, 3)), image[None]
+    )(wave_field, source_field, *tables, omegas, velocities, lower_ref[0], blend_weight[0])
+    return out, image.T[None]
 
 
 def solution(mesh):

time: 54 us -> 48.2 us (0.89)
  local copies, waits for them, and re-layouts: 7.4 us -> 3.18 us
  Pallas kernels: 45.7 us -> 44.2 us
    unnamed x8 -> x4, local copies, waits for them, and re-layouts: 7.4 us -> 3.18 us
    pallas_call x1, Pallas kernels: 45.7 us -> 44.2 us  [on_device(): pl.pallas_call(functools.partial(kernel, dims), out_shape=(jax.ShapeDtype...]
where the time goes in v2:
time: 48.2 us; the launch traced here: 48.1 us
  Pallas kernels  44.2 us (92%)
  local copies, waits for them, and re-layouts  3.18 us (7%)
  between operations  0.65 us (1%)
    pallas_call x1, Pallas kernels, on_device(): pl.pallas_call(functools.partial(kernel, dims), out_shape=(jax.ShapeDtype...  44.2 us
    unnamed x4, local copies, waits for them, and re-layouts  3.18 us

profile of v2, /device:TPU:0, one launch (start us, length us, event | category | flops | bytes accessed | tf_op | source)
XLA Modules:
  0.0 48.1 jit_solution(11024526768467246735)
XLA Ops:
  0.6 44.2 %shard_map.131 = (f32[2,128,2,512]{3,2,1,0:T(2,128)}, f32[64,128]{1,0:T(8,128)}) custom-call(f32[2,128,2,512]{3,2,1,0:T(2,128)} %wave_ref.1, f32[1,2,128,2,512]{4,3,2,1,0:T(2,128)} %source_ref.1, bf16[2,256,256]{2,1,0:T(8,128)(2,1)} %constant.12.clone.high_fwd, bf16[2,256,256]{2,1,0:T(8,128)(2,1)} %constant.13.clone.low_fwd, ...), custom_call_target="tpu_custom_call" | custom-call | tf_op jit(solution)/shard_map/pallas_call | solution.py:402
  44.9 0.0 copy-start
  44.9 2.6 %copy.16 = f32[2,128,2,512]{3,2,1,0:T(2,128)} copy(f32[2,128,2,512]{3,2,1,0:T(2,128)} %get-tuple-element.8) | data formatting | bytes 2097152
  47.5 0.0 copy-done
  47.5 0.6 %copy.17 = f32[1,128,64]{1,2,0:T(8,128)} copy(f32[1,128,64]{1,2,0:T(8,128)S(1)} %bitcast.5) | data formatting | bytes 65536
Async XLA Ops:
  44.9 2.6 %copy-start = (f32[64,128]{1,0:T(8,128)S(1)}, f32[64,128]{1,0:T(8,128)}, u32[]{:S(2)}) copy-start(f32[64,128]{1,0:T(8,128)} %get-tuple-element.5) | copy-start | bytes 98308

commit v3 on v2

--- a/solution.py
+++ b/solution.py
@@ -377,6 +377,23 @@
         copy.wait_send()
     for _, _, copy in image_copies:
         copy.wait_send()
+
+
+def settle(from_field, from_image, field, image, sem, image_sem):
+    freqs, rows = field.shape[:2]
+    parts = 4
+    step = rows // parts
+    copies = [pltpu.make_async_copy(from_image, image, image_sem)]
+    for f in range(freqs):
+        for i in range(parts):
+            span = pl.ds(i * step, step)
+            copies.append(
+                pltpu.make_async_copy(from_field.at[f, span], field.at[f, span], sem.at[f, i])
+            )
+    for copy in copies:
+        copy.start()
+    for copy in copies:
+        copy.wait()
 
 
 def on_device(wave_field, source_field, omegas, velocities, lower_ref, blend_weight):
@@ -440,6 +457,17 @@
             collective_id=0, has_side_effects=True, vmem_limit_bytes=56 * 1024 * 1024
         ),
     )(wave_field, source_field, *tables, omegas, velocities, lower_ref[0], blend_weight[0])
+    out, image = pl.pallas_call(
+        settle,
+        out_shape=(
+            jax.ShapeDtypeStruct(out.shape, f32),
+            jax.ShapeDtypeStruct(image.shape, f32),
+        ),
+        in_specs=[hbm, hbm],
+        out_specs=(hbm, hbm),
+        scratch_shapes=[pltpu.SemaphoreType.DMA((freqs, 4)), pltpu.SemaphoreType.DMA],
+        compiler_params=pltpu.CompilerParams(has_side_effects=True),
+    )(out, image)
     return out, image.T[None]
 
 

time: 48.2 us -> 79.1 us (1.64)
  Pallas kernels: 44.2 us -> 78.2 us
  local copies, waits for them, and re-layouts: 3.18 us -> 0 us
    pallas_call x0 -> x1, Pallas kernels: none -> 33.9 us  [on_device(): pl.pallas_call(settle, out_shape=(jax.ShapeDtypeStruct(out.shape, f32), j...]
    unnamed x4 -> x0, local copies, waits for them, and re-layouts: 3.18 us -> none
where the time goes in v3:
time: 79.1 us; the launch traced here: 79 us
  Pallas kernels  78.2 us (99%)
  between operations  0.8 us (1%)
    pallas_call x1, Pallas kernels, on_device(): pl.pallas_call(functools.partial(kernel, dims), out_shape=(jax.ShapeDtype...  44.2 us
    pallas_call x1, Pallas kernels, on_device(): pl.pallas_call(settle, out_shape=(jax.ShapeDtypeStruct(out.shape, f32), j...  33.9 us

profile of v3, /device:TPU:0, one launch (start us, length us, event | category | flops | bytes accessed | tf_op | source)
XLA Modules:
  0.0 79.0 jit_solution(6873751783081953708)
XLA Ops:
  0.6 44.2 %shard_map.131 = (f32[2,128,2,512]{3,2,1,0:T(2,128)}, f32[64,128]{1,0:T(8,128)}) custom-call(f32[2,128,2,512]{3,2,1,0:T(2,128)} %wave_ref.1, f32[1,2,128,2,512]{4,3,2,1,0:T(2,128)} %source_ref.1, bf16[2,256,256]{2,1,0:T(8,128)(2,1)} %constant.12.clone.high_fwd, bf16[2,256,256]{2,1,0:T(8,128)(2,1)} %constant.13.clone.low_fwd, ...), custom_call_target="tpu_custom_call" | custom-call | tf_op jit(solution)/shard_map/pallas_call | solution.py:419
  44.9 33.9 %shard_map.132 = (f32[2,128,2,512]{3,2,1,0:T(2,128)}, f32[64,128]{1,0:T(8,128)}) custom-call(f32[2,128,2,512]{3,2,1,0:T(2,128)} %get-tuple-element.6.from_field, f32[64,128]{1,0:T(8,128)} %get-tuple-element.7.from_image), custom_call_target="tpu_custom_call" | custom-call | tf_op jit(solution)/shard_map/pallas_call | solution.py:460
